TPU v7x, 32 devices: a whole 2x2x4 slice. The times are simulated.
32 devices in a mesh: dom: 4 (over y, core), spec: 8 (over z, x).
Axes of the slice: x: 2, y: 2, z: 4, core: 2. Of those that a mesh axis runs over, the one named last changes fastest.
Arguments:
- spectrum: float32 [256, 131072], P('spec', 'dom'), may hold values from -6 to 6
- conductance: float32 [256, 131072], P(None, ('dom', 'spec')), may hold values from 0.05 to 2
- capacitance: float32 [256, 131072], P(None, ('dom', 'spec')), may hold values from 0.05 to 2
- block_cond: float32 [1024, 128, 128], P(('dom', 'spec')), may hold values from -0.5 to 0.5
- block_cap: float32 [1024, 128, 128], P(('dom', 'spec')), may hold values from -0.5 to 0.5
- boundary_nodes: int32 [4, 128], P('dom'), may hold values from 0 to 32767, as said below
- couple_src: int32 [4, 3], P('dom'), may hold values from 0 to 3, as said below
- couple_count: int32 [4], P('dom'), may hold values from 1 to 3, as said below
- couple_cond: float32 [4, 3, 128, 128], P('dom'), may hold values from -0.5 to 0.5
- couple_cap: float32 [4, 3, 128, 128], P('dom'), may hold values from -0.5 to 0.5
Outputs:
- jacobian_product: float32 [256, 131072], P('spec', 'dom')
Inputs may be any that keep to these rules, and one draw needn't show every extreme that they name: `boundary_nodes`: row d lists 128 distinct nodes of partition d; entries 16 * s to 16 * (s + 1) - 1 lie among nodes 4096 * s to 4096 * (s + 1) - 1 and increase. `couple_src`: row d holds every partition other than d once. Partition d uses the first couple_count[d] entries of its rows of couple_src, couple_cond and couple_cap; some partition uses all 3.
All inputs are finite; a program needn't handle non-finite values.
Results may differ from a plain program's by a relative error of at most 0.0001.
Values sent between devices are 32-bit elements; how exact they have to be, the bound alone decides.
A program may use at most 192 MiB of HBM per device.

v0:
```python
import functools
import math

import jax
import jax.numpy as jnp
import ml_dtypes
import numpy as np
from jax import lax
from jax.experimental import pallas as pl
from jax.experimental.pallas import tpu as pltpu
from jax.sharding import PartitionSpec as P

MESH = pl.DeviceIdType.MESH
CHUNK = 512
GATHER = 2048
f32 = jnp.float32
bf16 = jnp.bfloat16


def split_table(table):
    high = table.astype(ml_dtypes.bfloat16)
    low = (table - high.astype(np.float64)).astype(ml_dtypes.bfloat16)
    return high, low


def fourier_tables(length):
    ids = np.arange(length)
    harmonic = np.where(ids == 1, length // 2, ids // 2)
    phase = (ids[:, None] * harmonic[None, :]) % length
    angles = phase * (2.0 * math.pi / length)
    is_sine = (ids % 2 == 1) & (ids >= 2)
    basis = np.where(is_sine[None, :], np.sin(angles), np.cos(angles))
    forward = basis.T * np.where(ids < 2, 1.0 / length, 2.0 / length)[:, None]
    frequency = np.where(ids >= 2, (ids // 2) * (2.0 / length), 0.0)[:, None]
    swapped = forward.reshape(length // 2, 2, length)[:, ::-1].reshape(length, length)
    slope = np.where((ids % 2 == 0)[:, None], frequency, -frequency) * swapped
    return split_table(basis) + split_table(np.concatenate([forward, slope], axis=1))


def split(values):
    high = values.astype(bf16)
    return high, (values - high.astype(f32)).astype(bf16)


def dot3(left, right, dims=(((1,), (0,)), ((), ()))):
    dot = functools.partial(lax.dot_general, dimension_numbers=dims, preferred_element_type=f32)
    return dot(left[0], right[0]) + (dot(left[0], right[1]) + dot(left[1], right[0]))


BOTH_LANES = (((1,), (1,)), ((), ()))


def derivative(values, first_row, length):
    rows = values.shape[0]
    ids = first_row + lax.broadcasted_iota(jnp.int32, (rows, 1), 0)
    frequency = (ids // 2).astype(f32) * (2.0 / length)
    even = ids % 2 == 0
    from_next = jnp.where(even, frequency, 0.0)
    from_last = jnp.where(even, 0.0, -frequency)
    return from_next * pltpu.roll(values, rows - 1, 0) + from_last * pltpu.roll(values, 1, 0)


def kernel(
    n_dom,
    n_spec,
    spectrum,
    cond,
    cap,
    block_cond,
    block_cap,
    bound,
    sources,
    used,
    couple_cond,
    couple_cap,
    basis_h,
    basis_l,
    fwd_h,
    fwd_l,
    out,
    x_all,
    y_all,
    o_all,
    spec_v,
    cond_v,
    cap_v,
    bcond_v,
    bcap_v,
    ccond_v,
    ccap_v,
    basis_hv,
    basis_lv,
    fwd_hv,
    fwd_lv,
    gathered,
    bound_col,
    current,
    load_sem,
    own_sem,
    keep_sem,
    out_sem,
    go_send,
    go_recv,
    back_send,
    back_recv,
    dom_send,
    dom_recv,
):
    rows = spectrum.shape[0]
    length, nodes = cond.shape
    n_bound = bound.shape[1]
    n_chunks = nodes // CHUNK
    dom = lax.axis_index("dom")
    me = lax.axis_index("spec")
    my_row = pl.multiple_of(me * rows, rows)

    def spec_peer(k):
        return lax.rem(me + k, n_spec)

    barrier = pltpu.get_barrier_semaphore()
    for k in range(1, n_spec):
        pl.semaphore_signal(barrier, inc=1, device_id=(dom, spec_peer(k)), device_id_type=MESH)
    for k in range(1, n_dom):
        pl.semaphore_signal(
            barrier, inc=1, device_id=(lax.rem(dom + k, n_dom), me), device_id_type=MESH
        )
    pl.semaphore_wait(barrier, n_spec - 1 + n_dom - 1)

    def lanes(first, size):
        return pl.ds(pl.multiple_of(first, size), size)

    def send_go(c, carry):
        for k in range(1, n_spec):
            peer = spec_peer(k)
            pltpu.make_async_remote_copy(
                src_ref=spectrum.at[:, lanes(peer * nodes + c * CHUNK, CHUNK)],
                dst_ref=x_all.at[pl.ds(my_row, rows), lanes(c * CHUNK, CHUNK)],
                send_sem=go_send,
                recv_sem=go_recv.at[c],
                device_id=(dom, peer),
                device_id_type=MESH,
            ).start()
        return carry

    lax.fori_loop(0, n_chunks, send_go, 0)

    loads = [
        pltpu.make_async_copy(source, target, load_sem.at[i])
        for i, (source, target) in enumerate(
            [
                (spectrum, spec_v),
                (couple_cond, ccond_v),
                (couple_cap, ccap_v),
                (basis_h, basis_hv),
                (basis_l, basis_lv),
                (fwd_h, fwd_hv),
                (fwd_l, fwd_lv),
                (cond, cond_v),
                (cap, cap_v),
                (block_cond, bcond_v),
                (block_cap, bcap_v),
            ]
        )
    ]
    own = pltpu.make_async_copy(
        spectrum.at[:, lanes(me * nodes, nodes)], x_all.at[pl.ds(my_row, rows), :], own_sem
    )
    for copy in loads:
        copy.start()
    own.start()

    square = (n_bound, n_bound)
    diagonal = lax.broadcasted_iota(jnp.int32, square, 0) == lax.broadcasted_iota(
        jnp.int32, square, 1
    )
    spread = jnp.broadcast_to(bound[...], square)
    bound_col[...] = jnp.sum(jnp.where(diagonal, spread.astype(f32), 0.0), axis=1, keepdims=True)

    def one_hot(first, size):
        ids = (first + lax.broadcasted_iota(jnp.int32, (n_bound, size), 1)).astype(f32)
        return jnp.where(ids == bound_col[...], 1.0, 0.0).astype(bf16)

    loads[0].wait()

    def pick(i, total):
        columns = lanes(i * GATHER, GATHER)
        high, low = split(spec_v[:, columns])
        both = jnp.concatenate([high, low], axis=0)
        return total + lax.dot_general(
            both, one_hot(i * GATHER, GATHER), BOTH_LANES, preferred_element_type=f32
        )

    picked = lax.fori_loop(
        0, spectrum.shape[1] // GATHER, pick, jnp.zeros((2 * rows, n_bound), f32)
    )
    gathered[dom] = picked[:rows] + picked[rows:]
    for k in range(1, n_dom):
        pltpu.make_async_remote_copy(
            src_ref=gathered.at[dom],
            dst_ref=gathered.at[dom],
            send_sem=dom_send,
            recv_sem=dom_recv,
            device_id=(lax.rem(dom + k, n_dom), me),
            device_id_type=MESH,
        ).start()

    for copy in loads[1:]:
        copy.wait()
    own.wait()

    def work(c, carry):
        columns = lanes(c * CHUNK, CHUNK)
        arrived = x_all.at[pl.ds(0, (n_spec - 1) * rows), columns]
        pltpu.make_async_copy(arrived, arrived, go_recv.at[c]).wait()
        x = x_all[:, columns]
        wave = dot3((basis_hv[...], basis_lv[...]), split(x))
        both = jnp.concatenate([cond_v[:, columns] * wave, cap_v[:, columns] * wave], axis=0)
        y = dot3((fwd_hv[...], fwd_lv[...]), split(both))
        slope = derivative(x, 0, length)
        size = bcond_v.shape[1]
        parts = []
        for b in range(CHUNK // size):
            block = c * (CHUNK // size) + b
            here = slice(b * size, (b + 1) * size)
            pair = jnp.concatenate([x[:, here], slope[:, here]], axis=1)
            matrix = jnp.concatenate([bcond_v[block], bcap_v[block]], axis=1)
            parts.append(y[:, here] + dot3(split(pair), split(matrix), BOTH_LANES))
        y_all[:, columns] = jnp.concatenate(parts, axis=1)
        target = lanes(me * nodes + c * CHUNK, CHUNK)
        for k in range(1, n_spec):
            peer = spec_peer(k)
            pltpu.make_async_remote_copy(
                src_ref=y_all.at[pl.ds(pl.multiple_of(peer * rows, rows), rows), columns],
                dst_ref=o_all.at[:, target],
                send_sem=back_send,
                recv_sem=back_recv.at[c],
                device_id=(dom, peer),
                device_id_type=MESH,
            ).start()
        pltpu.make_async_copy(
            y_all.at[pl.ds(my_row, rows), columns], o_all.at[:, target], keep_sem.at[c]
        ).start()
        return carry

    lax.fori_loop(0, n_chunks, work, 0)

    others = gathered.at[pl.ds(0, n_dom - 1)]
    pltpu.make_async_copy(others, others, dom_recv).wait()
    total = jnp.zeros((rows, n_bound), f32)
    for c in range(sources.shape[1]):
        value = jnp.zeros((rows, n_bound), f32)
        for p in range(n_dom):
            chosen = jnp.where((sources[0, c] == p) & (c < used[0]), 1.0, 0.0)
            value = value + chosen * gathered[p]
        slope = derivative(value, me * rows, length)
        total = total + dot3(split(value), split(ccond_v[c]), BOTH_LANES)
        total = total + dot3(split(slope), split(ccap_v[c]), BOTH_LANES)
    current[...] = total

    def finish(c, carry):
        every = o_all.at[:, pl.ds(0, (n_spec - 1) * CHUNK)]
        pltpu.make_async_copy(every, every, back_recv.at[c]).wait()
        kept = o_all.at[:, pl.ds(0, CHUNK)]
        pltpu.make_async_copy(kept, kept, keep_sem.at[c]).wait()
        high, low = split(current[...])
        for s in range(n_spec):
            first = s * nodes + c * CHUNK
            columns = lanes(first, CHUNK)
            chosen = one_hot(first, CHUNK)
            o_all[:, columns] += jnp.dot(high, chosen, preferred_element_type=f32) + jnp.dot(
                low, chosen, preferred_element_type=f32
            )
            pltpu.make_async_copy(o_all.at[:, columns], out.at[:, columns], out_sem).start()
        return carry

    lax.fori_loop(0, n_chunks, finish, 0)

    pltpu.make_async_copy(o_all, out, out_sem).wait()
    sent = spectrum.at[:, pl.ds(0, (n_spec - 1) * nodes)]
    pltpu.make_async_copy(sent, sent, go_send).wait()
    sent = y_all.at[pl.ds(0, (n_spec - 1) * rows), :]
    pltpu.make_async_copy(sent, sent, back_send).wait()
    pltpu.make_async_copy(others, others, dom_send).wait()


def solution(mesh):
    n_dom, n_spec = mesh.shape["dom"], mesh.shape["spec"]

    def shards(
        spectrum,
        cond,
        cap,
        block_cond,
        block_cap,
        bound,
        sources,
        used,
        couple_cond,
        couple_cap,
    ):
        rows = spectrum.shape[0]
        length, nodes = cond.shape
        n_bound = bound.shape[1]
        n_chunks = nodes // CHUNK
        tables = [jnp.asarray(t) for t in fourier_tables(length)]
        couple_cond, couple_cap = couple_cond[0], couple_cap[0]
        anywhere = pl.BlockSpec(memory_space=pl.ANY)
        vmem = pl.BlockSpec(memory_space=pltpu.VMEM)
        smem = pl.BlockSpec(memory_space=pltpu.SMEM)
        dma = pltpu.SemaphoreType.DMA
        return pl.pallas_call(
            functools.partial(kernel, n_dom, n_spec),
            out_shape=jax.ShapeDtypeStruct(spectrum.shape, f32),
            in_specs=[anywhere] * 5 + [vmem, smem, smem] + [anywhere] * 6,
            out_specs=anywhere,
            scratch_shapes=[
                pltpu.VMEM((length, nodes), f32),
                pltpu.VMEM((length, nodes), f32),
                pltpu.VMEM(spectrum.shape, f32),
                pltpu.VMEM(spectrum.shape, f32),
                pltpu.VMEM(cond.shape, f32),
                pltpu.VMEM(cap.shape, f32),
                pltpu.VMEM(block_cond.shape, f32),
                pltpu.VMEM(block_cap.shape, f32),
                pltpu.VMEM(couple_cond.shape, f32),
                pltpu.VMEM(couple_cap.shape, f32),
            ]
            + [pltpu.VMEM(t.shape, bf16) for t in tables]
            + [
                pltpu.VMEM((n_dom, rows, n_bound), f32),
                pltpu.VMEM((n_bound, 1), f32),
                pltpu.VMEM((rows, n_bound), f32),
                dma((11,)),
                dma,
                dma((n_chunks,)),
                dma,
                dma,
                dma((n_chunks,)),
                dma,
                dma((n_chunks,)),
                dma,
                dma,
            ],
            compiler_params=pltpu.CompilerParams(
                collective_id=0, has_side_effects=True, vmem_limit_bytes=56 * 1024 * 1024
            ),
            cost_estimate=pl.CostEstimate(
                flops=6 * length * nodes * (4 * length), bytes_accessed=20 << 20, transcendentals=0
            ),
        )(
            spectrum,
            cond,
            cap,
            block_cond,
            block_cap,
            bound,
            sources,
            used,
            couple_cond,
            couple_cap,
            *tables,
        )

    return jax.shard_map(
        shards,
        mesh=mesh,
        in_specs=(
            P("spec", "dom"),
            P(None, ("dom", "spec")),
            P(None, ("dom", "spec")),
            P(("dom", "spec"), None, None),
            P(("dom", "spec"), None, None),
            P("dom", None),
            P("dom", None),
            P("dom"),
            P("dom", None, None, None),
            P("dom", None, None, None),
        ),
        out_specs=P("spec", "dom"),
        check_vma=False,
    )
```

profile of v0, /device:TPU:15, one launch (start us, length us, event | category | flops | bytes accessed | tf_op | source)
XLA Modules:
  0.0 192.4 jit_solution(14308033032967837144)
XLA Ops:
  0.7 187.2 %shard_map.136 = f32[32,32768]{1,0:T(8,128)} custom-call(f32[32,32768]{1,0:T(8,128)} %spectrum.1, f32[256,4096]{1,0:T(8,128)} %cond.1, f32[256,4096]{1,0:T(8,128)} %cap.1, f32[32,128,128]{2,1,0:T(8,128)} %block_cond.1, f32[32,128,128]{2,1,0:T(8,128)} %block_cap.1, s32[1,128]{1,0:T(1,128)} %bound.1, s32[1,3]{1,0:T(1,128)} %sources.1, s32[1]{0:T(128)S(6)} %copy.16.used, ...), custom_call_target="tpu_custom_call" | custom-call | flops 6442450944 | bytes 20971520 | tf_op jit(solution)/shard_map/pallas_call | solution.py:311
  187.9 4.5 %copy.17 = f32[32,32768]{1,0:T(8,128)} copy(f32[32,32768]{1,0:T(8,128)} %shard_map.136) | data formatting | bytes 8388608
where the time goes:
time: 193 us; the launch traced here: 192 us
  Pallas kernels  187 us (97%)
  local copies, waits for them, and re-layouts  4.47 us (2%)
    pallas_call x1, Pallas kernels, shards(): pl.pallas_call(functools.partial(kernel, n_dom, n_spec), out_shape=jax.Sh...  187 us
    unnamed x1, local copies, waits for them, and re-layouts  4.47 us

commit v1 on v0

--- a/solution.py
+++ b/solution.py
@@ -77,10 +77,9 @@
     basis_l,
     fwd_h,
     fwd_l,
-    out,
+    o_all,
     x_all,
     y_all,
-    o_all,
     spec_v,
     cond_v,
     cap_v,
@@ -98,7 +97,6 @@
     load_sem,
     own_sem,
     keep_sem,
-    out_sem,
     go_send,
     go_recv,
     back_send,
@@ -124,25 +122,8 @@
         pl.semaphore_signal(
             barrier, inc=1, device_id=(lax.rem(dom + k, n_dom), me), device_id_type=MESH
         )
-    pl.semaphore_wait(barrier, n_spec - 1 + n_dom - 1)
-
     def lanes(first, size):
         return pl.ds(pl.multiple_of(first, size), size)
-
-    def send_go(c, carry):
-        for k in range(1, n_spec):
-            peer = spec_peer(k)
-            pltpu.make_async_remote_copy(
-                src_ref=spectrum.at[:, lanes(peer * nodes + c * CHUNK, CHUNK)],
-                dst_ref=x_all.at[pl.ds(my_row, rows), lanes(c * CHUNK, CHUNK)],
-                send_sem=go_send,
-                recv_sem=go_recv.at[c],
-                device_id=(dom, peer),
-                device_id_type=MESH,
-            ).start()
-        return carry
-
-    lax.fori_loop(0, n_chunks, send_go, 0)
 
     loads = [
         pltpu.make_async_copy(source, target, load_sem.at[i])
@@ -168,6 +149,23 @@
     for copy in loads:
         copy.start()
     own.start()
+
+    pl.semaphore_wait(barrier, n_spec - 1 + n_dom - 1)
+
+    def send_go(c, carry):
+        for k in range(1, n_spec):
+            peer = spec_peer(k)
+            pltpu.make_async_remote_copy(
+                src_ref=spectrum.at[:, lanes(peer * nodes + c * CHUNK, CHUNK)],
+                dst_ref=x_all.at[pl.ds(my_row, rows), lanes(c * CHUNK, CHUNK)],
+                send_sem=go_send,
+                recv_sem=go_recv.at[c],
+                device_id=(dom, peer),
+                device_id_type=MESH,
+            ).start()
+        return carry
+
+    lax.fori_loop(0, n_chunks, send_go, 0)
 
     square = (n_bound, n_bound)
     diagonal = lax.broadcasted_iota(jnp.int32, square, 0) == lax.broadcasted_iota(
@@ -257,25 +255,29 @@
         total = total + dot3(split(slope), split(ccap_v[c]), BOTH_LANES)
     current[...] = total
 
+    def place(i, carry):
+        columns = lanes(i * GATHER, GATHER)
+        high, low = split(current[...])
+        chosen = one_hot(i * GATHER, GATHER)
+        spec_v[:, columns] = jnp.dot(high, chosen, preferred_element_type=f32) + jnp.dot(
+            low, chosen, preferred_element_type=f32
+        )
+        return carry
+
+    lax.fori_loop(0, spectrum.shape[1] // GATHER, place, 0)
+
     def finish(c, carry):
         every = o_all.at[:, pl.ds(0, (n_spec - 1) * CHUNK)]
         pltpu.make_async_copy(every, every, back_recv.at[c]).wait()
         kept = o_all.at[:, pl.ds(0, CHUNK)]
         pltpu.make_async_copy(kept, kept, keep_sem.at[c]).wait()
-        high, low = split(current[...])
         for s in range(n_spec):
-            first = s * nodes + c * CHUNK
-            columns = lanes(first, CHUNK)
-            chosen = one_hot(first, CHUNK)
-            o_all[:, columns] += jnp.dot(high, chosen, preferred_element_type=f32) + jnp.dot(
-                low, chosen, preferred_element_type=f32
-            )
-            pltpu.make_async_copy(o_all.at[:, columns], out.at[:, columns], out_sem).start()
+            columns = lanes(s * nodes + c * CHUNK, CHUNK)
+            o_all[:, columns] += spec_v[:, columns]
         return carry
 
     lax.fori_loop(0, n_chunks, finish, 0)
 
-    pltpu.make_async_copy(o_all, out, out_sem).wait()
     sent = spectrum.at[:, pl.ds(0, (n_spec - 1) * nodes)]
     pltpu.make_async_copy(sent, sent, go_send).wait()
     sent = y_all.at[pl.ds(0, (n_spec - 1) * rows), :]
@@ -310,13 +312,12 @@
         dma = pltpu.SemaphoreType.DMA
         return pl.pallas_call(
             functools.partial(kernel, n_dom, n_spec),
-            out_shape=jax.ShapeDtypeStruct(spectrum.shape, f32),
+            out_shape=pltpu.VMEM(spectrum.shape, f32),
             in_specs=[anywhere] * 5 + [vmem, smem, smem] + [anywhere] * 6,
-            out_specs=anywhere,
+            out_specs=vmem,
             scratch_shapes=[
                 pltpu.VMEM((length, nodes), f32),
                 pltpu.VMEM((length, nodes), f32),
-                pltpu.VMEM(spectrum.shape, f32),
                 pltpu.VMEM(spectrum.shape, f32),
                 pltpu.VMEM(cond.shape, f32),
                 pltpu.VMEM(cap.shape, f32),
@@ -333,7 +334,6 @@
                 dma((11,)),
                 dma,
                 dma((n_chunks,)),
-                dma,
                 dma,
                 dma((n_chunks,)),
                 dma,

time: 193 us -> 189 us (0.979)
  local copies, waits for them, and re-layouts: 4.47 us -> 2.02 us
    unnamed x1, local copies, waits for them, and re-layouts: 4.47 us -> 2.02 us
where the time goes in v1:
time: 189 us
  Pallas kernels  186 us (98%)
  local copies, waits for them, and re-layouts  2.02 us (1%)
    pallas_call x1, Pallas kernels, shards(): pl.pallas_call(functools.partial(kernel, n_dom, n_spec), out_shape=pltpu....  186 us

profile of v1, /device:TPU:15, one launch (start us, length us, event | category | flops | bytes accessed | tf_op | source)
XLA Modules:
  0.0 188.8 jit_solution(204253990498410247)
XLA Ops:
  0.7 186.2 %shard_map.136 = f32[32,32768]{1,0:T(8,128)S(1)} custom-call(f32[32,32768]{1,0:T(8,128)} %spectrum.1, f32[256,4096]{1,0:T(8,128)} %cond.1, f32[256,4096]{1,0:T(8,128)} %cap.1, f32[32,128,128]{2,1,0:T(8,128)} %block_cond.1, f32[32,128,128]{2,1,0:T(8,128)} %block_cap.1, s32[1,128]{1,0:T(1,128)} %bound.1, s32[1,3]{1,0:T(1,128)} %sources.1, s32[1]{0:T(128)S(6)} %copy.17.used, ...), custom_call_target="tpu_custom_call" | custom-call | flops 6442450944 | bytes 20971520 | tf_op jit(solution)/shard_map/pallas_call | solution.py:313
  186.8 2.0 %copy.16 = f32[32,32768]{1,0:T(8,128)} copy(f32[32,32768]{1,0:T(8,128)S(1)} %shard_map.136) | data formatting | bytes 8388608

commit v2 on v1

--- a/solution.py
+++ b/solution.py
@@ -115,6 +115,14 @@
     def spec_peer(k):
         return lax.rem(me + k, n_spec)
 
+    half = n_spec // 2
+    side, place_in_half = me // half, lax.rem(me, half)
+    far = [(1 - side) * half + lax.rem(place_in_half + i, half) for i in range(half)]
+    near = [side * half + lax.rem(place_in_half + i, half) for i in range(1, half)]
+    mixed = [far[0]]
+    for one, other in zip(near, far[1:]):
+        mixed += [one, other]
+
     barrier = pltpu.get_barrier_semaphore()
     for k in range(1, n_spec):
         pl.semaphore_signal(barrier, inc=1, device_id=(dom, spec_peer(k)), device_id_type=MESH)
@@ -152,20 +160,29 @@
 
     pl.semaphore_wait(barrier, n_spec - 1 + n_dom - 1)
 
-    def send_go(c, carry):
-        for k in range(1, n_spec):
-            peer = spec_peer(k)
-            pltpu.make_async_remote_copy(
-                src_ref=spectrum.at[:, lanes(peer * nodes + c * CHUNK, CHUNK)],
-                dst_ref=x_all.at[pl.ds(my_row, rows), lanes(c * CHUNK, CHUNK)],
-                send_sem=go_send,
-                recv_sem=go_recv.at[c],
-                device_id=(dom, peer),
-                device_id_type=MESH,
-            ).start()
+    def send_go(peer, c):
+        pltpu.make_async_remote_copy(
+            src_ref=spectrum.at[:, lanes(peer * nodes + c * CHUNK, CHUNK)],
+            dst_ref=x_all.at[pl.ds(my_row, rows), lanes(c * CHUNK, CHUNK)],
+            send_sem=go_send,
+            recv_sem=go_recv.at[c],
+            device_id=(dom, peer),
+            device_id_type=MESH,
+        ).start()
+
+    for peer in far:
+        send_go(peer, 0)
+
+    def send_both(c, carry):
+        send_go(far[0], c + 1)
+        for one, other in zip(near, far[1:]):
+            send_go(one, c)
+            send_go(other, c + 1)
         return carry
 
-    lax.fori_loop(0, n_chunks, send_go, 0)
+    lax.fori_loop(0, n_chunks - 1, send_both, 0)
+    for peer in near:
+        send_go(peer, n_chunks - 1)
 
     square = (n_bound, n_bound)
     diagonal = lax.broadcasted_iota(jnp.int32, square, 0) == lax.broadcasted_iota(
@@ -225,8 +242,7 @@
             parts.append(y[:, here] + dot3(split(pair), split(matrix), BOTH_LANES))
         y_all[:, columns] = jnp.concatenate(parts, axis=1)
         target = lanes(me * nodes + c * CHUNK, CHUNK)
-        for k in range(1, n_spec):
-            peer = spec_peer(k)
+        for peer in mixed:
             pltpu.make_async_remote_copy(
                 src_ref=y_all.at[pl.ds(pl.multiple_of(peer * rows, rows), rows), columns],
                 dst_ref=o_all.at[:, target],

time: 189 us -> 192 us (1.016); the launches traced: 189 us -> 189 us
  no operation moved by 1% of the time
where the time goes in v2:
time: 192 us; the launch traced here: 189 us
  Pallas kernels  186 us (97%)
  local copies, waits for them, and re-layouts  2.02 us (1%)
    pallas_call x1, Pallas kernels, shards(): pl.pallas_call(functools.partial(kernel, n_dom, n_spec), out_shape=pltpu....  186 us

profile of v2, /device:TPU:15, one launch (start us, length us, event | category | flops | bytes accessed | tf_op | source)
XLA Modules:
  0.0 188.8 jit_solution(3433953651114151631)
XLA Ops:
  0.7 186.2 %shard_map.136 = f32[32,32768]{1,0:T(8,128)S(1)} custom-call(f32[32,32768]{1,0:T(8,128)} %spectrum.1, f32[256,4096]{1,0:T(8,128)} %cond.1, f32[256,4096]{1,0:T(8,128)} %cap.1, f32[32,128,128]{2,1,0:T(8,128)} %block_cond.1, f32[32,128,128]{2,1,0:T(8,128)} %block_cap.1, s32[1,128]{1,0:T(1,128)} %bound.1, s32[1,3]{1,0:T(1,128)} %sources.1, s32[1]{0:T(128)S(6)} %copy.17.used, ...), custom_call_target="tpu_custom_call" | custom-call | flops 6442450944 | bytes 20971520 | tf_op jit(solution)/shard_map/pallas_call | solution.py:329
  186.8 2.0 %copy.16 = f32[32,32768]{1,0:T(8,128)} copy(f32[32,32768]{1,0:T(8,128)S(1)} %shard_map.136) | data formatting | bytes 8388608

commit v3 on v1

--- a/solution.py
+++ b/solution.py
@@ -3,7 +3,6 @@
 
 import jax
 import jax.numpy as jnp
-import ml_dtypes
 import numpy as np
 from jax import lax
 from jax.experimental import pallas as pl
@@ -12,15 +11,10 @@
 
 MESH = pl.DeviceIdType.MESH
 CHUNK = 512
+AHEAD = 3
 GATHER = 2048
 f32 = jnp.float32
 bf16 = jnp.bfloat16
-
-
-def split_table(table):
-    high = table.astype(ml_dtypes.bfloat16)
-    low = (table - high.astype(np.float64)).astype(ml_dtypes.bfloat16)
-    return high, low
 
 
 def fourier_tables(length):
@@ -34,7 +28,8 @@
     frequency = np.where(ids >= 2, (ids // 2) * (2.0 / length), 0.0)[:, None]
     swapped = forward.reshape(length // 2, 2, length)[:, ::-1].reshape(length, length)
     slope = np.where((ids % 2 == 0)[:, None], frequency, -frequency) * swapped
-    return split_table(basis) + split_table(np.concatenate([forward, slope], axis=1))
+    both = np.concatenate([forward, slope], axis=1)
+    return basis.astype(np.float32), both.astype(np.float32)
 
 
 def split(values):
@@ -73,10 +68,8 @@
     used,
     couple_cond,
     couple_cap,
-    basis_h,
-    basis_l,
-    fwd_h,
-    fwd_l,
+    basis,
+    forward,
     o_all,
     x_all,
     y_all,
@@ -87,6 +80,8 @@
     bcap_v,
     ccond_v,
     ccap_v,
+    basis_v,
+    forward_v,
     basis_hv,
     basis_lv,
     fwd_hv,
@@ -132,10 +127,8 @@
                 (spectrum, spec_v),
                 (couple_cond, ccond_v),
                 (couple_cap, ccap_v),
-                (basis_h, basis_hv),
-                (basis_l, basis_lv),
-                (fwd_h, fwd_hv),
-                (fwd_l, fwd_lv),
+                (basis, basis_v),
+                (forward, forward_v),
                 (cond, cond_v),
                 (cap, cap_v),
                 (block_cond, bcond_v),
@@ -165,7 +158,8 @@
             ).start()
         return carry
 
-    lax.fori_loop(0, n_chunks, send_go, 0)
+    ahead = min(AHEAD, n_chunks)
+    lax.fori_loop(0, ahead, send_go, 0)
 
     square = (n_bound, n_bound)
     diagonal = lax.broadcasted_iota(jnp.int32, square, 0) == lax.broadcasted_iota(
@@ -205,11 +199,18 @@
     for copy in loads[1:]:
         copy.wait()
     own.wait()
+    basis_hv[...], basis_lv[...] = split(basis_v[...])
+    fwd_hv[...], fwd_lv[...] = split(forward_v[...])
 
     def work(c, carry):
         columns = lanes(c * CHUNK, CHUNK)
         arrived = x_all.at[pl.ds(0, (n_spec - 1) * rows), columns]
         pltpu.make_async_copy(arrived, arrived, go_recv.at[c]).wait()
+
+        @pl.when(c + ahead < n_chunks)
+        def _():
+            send_go(c + ahead, 0)
+
         x = x_all[:, columns]
         wave = dot3((basis_hv[...], basis_lv[...]), split(x))
         both = jnp.concatenate([cond_v[:, columns] * wave, cap_v[:, columns] * wave], axis=0)
@@ -313,7 +314,7 @@
         return pl.pallas_call(
             functools.partial(kernel, n_dom, n_spec),
             out_shape=pltpu.VMEM(spectrum.shape, f32),
-            in_specs=[anywhere] * 5 + [vmem, smem, smem] + [anywhere] * 6,
+            in_specs=[anywhere] * 5 + [vmem, smem, smem] + [anywhere] * 4,
             out_specs=vmem,
             scratch_shapes=[
                 pltpu.VMEM((length, nodes), f32),
@@ -326,12 +327,13 @@
                 pltpu.VMEM(couple_cond.shape, f32),
                 pltpu.VMEM(couple_cap.shape, f32),
             ]
-            + [pltpu.VMEM(t.shape, bf16) for t in tables]
+            + [pltpu.VMEM(t.shape, f32) for t in tables]
+            + [pltpu.VMEM(t.shape, bf16) for t in tables for _ in range(2)]
             + [
                 pltpu.VMEM((n_dom, rows, n_bound), f32),
                 pltpu.VMEM((n_bound, 1), f32),
                 pltpu.VMEM((rows, n_bound), f32),
-                dma((11,)),
+                dma((9,)),
                 dma,
                 dma((n_chunks,)),
                 dma,

time: 189 us -> 189 us (level)
  no operation moved by 1% of the time
where the time goes in v3:
time: 189 us
  Pallas kernels  186 us (98%)
  local copies, waits for them, and re-layouts  2.02 us (1%)
    pallas_call x1, Pallas kernels, shards(): pl.pallas_call(functools.partial(kernel, n_dom, n_spec), out_shape=pltpu....  186 us

profile of v3, /device:TPU:15, one launch (start us, length us, event | category | flops | bytes accessed | tf_op | source)
XLA Modules:
  0.0 189.1 jit_solution(2035467782435943343)
XLA Ops:
  0.7 186.4 %shard_map.118 = f32[32,32768]{1,0:T(8,128)S(1)} custom-call(f32[32,32768]{1,0:T(8,128)} %spectrum.1, f32[256,4096]{1,0:T(8,128)} %cond.1, f32[256,4096]{1,0:T(8,128)} %cap.1, f32[32,128,128]{2,1,0:T(8,128)} %block_cond.1, f32[32,128,128]{2,1,0:T(8,128)} %block_cap.1, s32[1,128]{1,0:T(1,128)} %bound.1, s32[1,3]{1,0:T(1,128)} %sources.1, s32[1]{0:T(128)S(6)} %copy.15.used, ...), custom_call_target="tpu_custom_call" | custom-call | flops 6442450944 | bytes 20971520 | tf_op jit(solution)/shard_map/pallas_call | solution.py:314
  187.1 2.0 %copy.14 = f32[32,32768]{1,0:T(8,128)} copy(f32[32,32768]{1,0:T(8,128)S(1)} %shard_map.118) | data formatting | bytes 8388608

commit v4 on v3

--- a/solution.py
+++ b/solution.py
@@ -10,8 +10,8 @@
 from jax.sharding import PartitionSpec as P
 
 MESH = pl.DeviceIdType.MESH
-CHUNK = 512
-AHEAD = 3
+CHUNK = 1024
+AHEAD = 4
 GATHER = 2048
 f32 = jnp.float32
 bf16 = jnp.bfloat16

time: 189 us -> 190 us (level)
  no operation moved by 1% of the time
where the time goes in v4:
time: 190 us; the launch traced here: 189 us
  Pallas kernels  187 us (98%)
  local copies, waits for them, and re-layouts  2.02 us (1%)
    pallas_call x1, Pallas kernels, shards(): pl.pallas_call(functools.partial(kernel, n_dom, n_spec), out_shape=pltpu....  187 us

profile of v4, /device:TPU:15, one launch (start us, length us, event | category | flops | bytes accessed | tf_op | source)
XLA Modules:
  0.0 189.4 jit_solution(11605010000343343333)
XLA Ops:
  0.7 186.7 %shard_map.118 = f32[32,32768]{1,0:T(8,128)S(1)} custom-call(f32[32,32768]{1,0:T(8,128)} %spectrum.1, f32[256,4096]{1,0:T(8,128)} %cond.1, f32[256,4096]{1,0:T(8,128)} %cap.1, f32[32,128,128]{2,1,0:T(8,128)} %block_cond.1, f32[32,128,128]{2,1,0:T(8,128)} %block_cap.1, s32[1,128]{1,0:T(1,128)} %bound.1, s32[1,3]{1,0:T(1,128)} %sources.1, s32[1]{0:T(128)S(6)} %copy.15.used, ...), custom_call_target="tpu_custom_call" | custom-call | flops 6442450944 | bytes 20971520 | tf_op jit(solution)/shard_map/pallas_call | solution.py:314
  187.3 2.0 %copy.14 = f32[32,32768]{1,0:T(8,128)} copy(f32[32,32768]{1,0:T(8,128)S(1)} %shard_map.118) | data formatting | bytes 8388608

commit v5 on v4

--- a/solution.py
+++ b/solution.py
@@ -10,7 +10,7 @@
 from jax.sharding import PartitionSpec as P
 
 MESH = pl.DeviceIdType.MESH
-CHUNK = 1024
+CHUNK = 512
 AHEAD = 4
 GATHER = 2048
 f32 = jnp.float32
@@ -86,6 +86,9 @@
     basis_lv,
     fwd_hv,
     fwd_lv,
+    bound_v,
+    sources_v,
+    used_v,
     gathered,
     bound_col,
     current,
@@ -124,6 +127,7 @@
         pltpu.make_async_copy(source, target, load_sem.at[i])
         for i, (source, target) in enumerate(
             [
+                (bound, bound_v),
                 (spectrum, spec_v),
                 (couple_cond, ccond_v),
                 (couple_cap, ccap_v),
@@ -133,6 +137,8 @@
                 (cap, cap_v),
                 (block_cond, bcond_v),
                 (block_cap, bcap_v),
+                (sources, sources_v),
+                (used, used_v),
             ]
         )
     ]
@@ -161,18 +167,19 @@
     ahead = min(AHEAD, n_chunks)
     lax.fori_loop(0, ahead, send_go, 0)
 
+    loads[0].wait()
     square = (n_bound, n_bound)
     diagonal = lax.broadcasted_iota(jnp.int32, square, 0) == lax.broadcasted_iota(
         jnp.int32, square, 1
     )
-    spread = jnp.broadcast_to(bound[...], square)
+    spread = jnp.broadcast_to(bound_v[...], square)
     bound_col[...] = jnp.sum(jnp.where(diagonal, spread.astype(f32), 0.0), axis=1, keepdims=True)
 
     def one_hot(first, size):
         ids = (first + lax.broadcasted_iota(jnp.int32, (n_bound, size), 1)).astype(f32)
         return jnp.where(ids == bound_col[...], 1.0, 0.0).astype(bf16)
 
-    loads[0].wait()
+    loads[1].wait()
 
     def pick(i, total):
         columns = lanes(i * GATHER, GATHER)
@@ -196,7 +203,7 @@
             device_id_type=MESH,
         ).start()
 
-    for copy in loads[1:]:
+    for copy in loads[2:]:
         copy.wait()
     own.wait()
     basis_hv[...], basis_lv[...] = split(basis_v[...])
@@ -249,7 +256,7 @@
     for c in range(sources.shape[1]):
         value = jnp.zeros((rows, n_bound), f32)
         for p in range(n_dom):
-            chosen = jnp.where((sources[0, c] == p) & (c < used[0]), 1.0, 0.0)
+            chosen = jnp.where((sources_v[:, c : c + 1] == p) & (used_v[0] > c), 1.0, 0.0)
             value = value + chosen * gathered[p]
         slope = derivative(value, me * rows, length)
         total = total + dot3(split(value), split(ccond_v[c]), BOTH_LANES)
@@ -309,12 +316,11 @@
         couple_cond, couple_cap = couple_cond[0], couple_cap[0]
         anywhere = pl.BlockSpec(memory_space=pl.ANY)
         vmem = pl.BlockSpec(memory_space=pltpu.VMEM)
-        smem = pl.BlockSpec(memory_space=pltpu.SMEM)
         dma = pltpu.SemaphoreType.DMA
         return pl.pallas_call(
             functools.partial(kernel, n_dom, n_spec),
             out_shape=pltpu.VMEM(spectrum.shape, f32),
-            in_specs=[anywhere] * 5 + [vmem, smem, smem] + [anywhere] * 4,
+            in_specs=[anywhere] * 12,
             out_specs=vmem,
             scratch_shapes=[
                 pltpu.VMEM((length, nodes), f32),
@@ -330,10 +336,13 @@
             + [pltpu.VMEM(t.shape, f32) for t in tables]
             + [pltpu.VMEM(t.shape, bf16) for t in tables for _ in range(2)]
             + [
+                pltpu.VMEM(bound.shape, jnp.int32),
+                pltpu.VMEM(sources.shape, jnp.int32),
+                pltpu.SMEM((1,), jnp.int32),
                 pltpu.VMEM((n_dom, rows, n_bound), f32),
                 pltpu.VMEM((n_bound, 1), f32),
                 pltpu.VMEM((rows, n_bound), f32),
-                dma((9,)),
+                dma((12,)),
                 dma,
                 dma((n_chunks,)),
                 dma,

time: 190 us -> 188 us (0.989)
  no operation moved by 1% of the time
where the time goes in v5:
time: 188 us
  Pallas kernels  186 us (99%)
  local copies, waits for them, and re-layouts  2.02 us (1%)
    pallas_call x1, Pallas kernels, shards(): pl.pallas_call(functools.partial(kernel, n_dom, n_spec), out_shape=pltpu....  186 us

profile of v5, /device:TPU:15, one launch (start us, length us, event | category | flops | bytes accessed | tf_op | source)
XLA Modules:
  0.0 188.3 jit_solution(4865414368615440114)
XLA Ops:
  0.7 185.6 %shard_map.118 = f32[32,32768]{1,0:T(8,128)S(1)} custom-call(f32[32,32768]{1,0:T(8,128)} %spectrum.1, f32[256,4096]{1,0:T(8,128)} %cond.1, f32[256,4096]{1,0:T(8,128)} %cap.1, f32[32,128,128]{2,1,0:T(8,128)} %block_cond.1, f32[32,128,128]{2,1,0:T(8,128)} %block_cap.1, s32[1,128]{1,0:T(1,128)} %bound.1, s32[1,3]{1,0:T(1,128)} %sources.1, s32[1]{0:T(128)S(6)} %copy.15.used, ...), custom_call_target="tpu_custom_call" | custom-call | flops 6442450944 | bytes 20971520 | tf_op jit(solution)/shard_map/pallas_call | solution.py:320
  186.2 2.0 %copy.14 = f32[32,32768]{1,0:T(8,128)} copy(f32[32,32768]{1,0:T(8,128)S(1)} %shard_map.118) | data formatting | bytes 8388608

commit v6 on v5

--- a/solution.py
+++ b/solution.py
@@ -145,9 +145,7 @@
     own = pltpu.make_async_copy(
         spectrum.at[:, lanes(me * nodes, nodes)], x_all.at[pl.ds(my_row, rows), :], own_sem
     )
-    for copy in loads:
-        copy.start()
-    own.start()
+    loads[0].start()
 
     pl.semaphore_wait(barrier, n_spec - 1 + n_dom - 1)
 
@@ -165,7 +163,11 @@
         return carry
 
     ahead = min(AHEAD, n_chunks)
-    lax.fori_loop(0, ahead, send_go, 0)
+    send_go(0, 0)
+    own.start()
+    for copy in loads[1:]:
+        copy.start()
+    lax.fori_loop(1, ahead, send_go, 0)
 
     loads[0].wait()
     square = (n_bound, n_bound)

time: 188 us -> 188 us (level)
  no operation moved by 1% of the time
where the time goes in v6:
time: 188 us
  Pallas kernels  186 us (99%)
  local copies, waits for them, and re-layouts  2.02 us (1%)
    pallas_call x1, Pallas kernels, shards(): pl.pallas_call(functools.partial(kernel, n_dom, n_spec), out_shape=pltpu....  186 us

profile of v6, /device:TPU:15, one launch (start us, length us, event | category | flops | bytes accessed | tf_op | source)
XLA Modules:
  0.0 188.3 jit_solution(13600158280107114250)
XLA Ops:
  0.7 185.6 %shard_map.118 = f32[32,32768]{1,0:T(8,128)S(1)} custom-call(f32[32,32768]{1,0:T(8,128)} %spectrum.1, f32[256,4096]{1,0:T(8,128)} %cond.1, f32[256,4096]{1,0:T(8,128)} %cap.1, f32[32,128,128]{2,1,0:T(8,128)} %block_cond.1, f32[32,128,128]{2,1,0:T(8,128)} %block_cap.1, s32[1,128]{1,0:T(1,128)} %bound.1, s32[1,3]{1,0:T(1,128)} %sources.1, s32[1]{0:T(128)S(6)} %copy.15.used, ...), custom_call_target="tpu_custom_call" | custom-call | flops 6442450944 | bytes 20971520 | tf_op jit(solution)/shard_map/pallas_call | solution.py:322
  186.2 2.0 %copy.14 = f32[32,32768]{1,0:T(8,128)} copy(f32[32,32768]{1,0:T(8,128)S(1)} %shard_map.118) | data formatting | bytes 8388608

commit v7 on v6

--- a/solution.py
+++ b/solution.py
@@ -10,8 +10,8 @@
 from jax.sharding import PartitionSpec as P
 
 MESH = pl.DeviceIdType.MESH
-CHUNK = 512
-AHEAD = 4
+CHUNK = 256
+AHEAD = 8
 GATHER = 2048
 f32 = jnp.float32
 bf16 = jnp.bfloat16
@@ -114,7 +114,7 @@
         return lax.rem(me + k, n_spec)
 
     barrier = pltpu.get_barrier_semaphore()
-    for k in range(1, n_spec):
+    for k in sorted(range(1, n_spec), key=lambda k: abs(k - n_spec // 2)):
         pl.semaphore_signal(barrier, inc=1, device_id=(dom, spec_peer(k)), device_id_type=MESH)
     for k in range(1, n_dom):
         pl.semaphore_signal(

time: 188 us -> 189 us (level)
  no operation moved by 1% of the time
where the time goes in v7:
time: 189 us; the launch traced here: 188 us
  Pallas kernels  185 us (98%)
  local copies, waits for them, and re-layouts  2.02 us (1%)
    pallas_call x1, Pallas kernels, shards(): pl.pallas_call(functools.partial(kernel, n_dom, n_spec), out_shape=pltpu....  185 us

profile of v7, /device:TPU:15, one launch (start us, length us, event | category | flops | bytes accessed | tf_op | source)
XLA Modules:
  0.0 188.0 jit_solution(9017748781995239644)
XLA Ops:
  0.7 185.3 %shard_map.118 = f32[32,32768]{1,0:T(8,128)S(1)} custom-call(f32[32,32768]{1,0:T(8,128)} %spectrum.1, f32[256,4096]{1,0:T(8,128)} %cond.1, f32[256,4096]{1,0:T(8,128)} %cap.1, f32[32,128,128]{2,1,0:T(8,128)} %block_cond.1, f32[32,128,128]{2,1,0:T(8,128)} %block_cap.1, s32[1,128]{1,0:T(1,128)} %bound.1, s32[1,3]{1,0:T(1,128)} %sources.1, s32[1]{0:T(128)S(6)} %copy.15.used, ...), custom_call_target="tpu_custom_call" | custom-call | flops 6442450944 | bytes 20971520 | tf_op jit(solution)/shard_map/pallas_call | solution.py:322
  186.0 2.0 %copy.14 = f32[32,32768]{1,0:T(8,128)} copy(f32[32,32768]{1,0:T(8,128)S(1)} %shard_map.118) | data formatting | bytes 8388608

commit v8 on v6

--- a/solution.py
+++ b/solution.py
@@ -295,6 +295,20 @@
     pltpu.make_async_copy(others, others, dom_send).wait()
 
 
+def write_out(n_parts, held, out, sem):
+    size = held.shape[1] // n_parts
+    copies = [
+        pltpu.make_async_copy(
+            held.at[:, pl.ds(i * size, size)], out.at[:, pl.ds(i * size, size)], sem.at[i]
+        )
+        for i in range(n_parts)
+    ]
+    for copy in copies:
+        copy.start()
+    for copy in copies:
+        copy.wait()
+
+
 def solution(mesh):
     n_dom, n_spec = mesh.shape["dom"], mesh.shape["spec"]
 
@@ -319,7 +333,7 @@
         anywhere = pl.BlockSpec(memory_space=pl.ANY)
         vmem = pl.BlockSpec(memory_space=pltpu.VMEM)
         dma = pltpu.SemaphoreType.DMA
-        return pl.pallas_call(
+        held = pl.pallas_call(
             functools.partial(kernel, n_dom, n_spec),
             out_shape=pltpu.VMEM(spectrum.shape, f32),
             in_specs=[anywhere] * 12,
@@ -373,6 +387,13 @@
             couple_cap,
             *tables,
         )
+        return pl.pallas_call(
+            functools.partial(write_out, n_spec),
+            out_shape=jax.ShapeDtypeStruct(spectrum.shape, f32),
+            in_specs=[vmem],
+            out_specs=anywhere,
+            scratch_shapes=[dma((n_spec,))],
+        )(held)
 
     return jax.shard_map(
         shards,

time: 188 us -> 193 us (1.027)
  Pallas kernels: 186 us -> 190 us
    pallas_call x0 -> x1, Pallas kernels: none -> 4.25 us  [shards(): pl.pallas_call(functools.partial(write_out, n_spec), out_shape=jax.ShapeD...]
where the time goes in v8:
time: 193 us; the launch traced here: 192 us
  Pallas kernels  190 us (98%)
  local copies, waits for them, and re-layouts  1.93 us (1%)
    pallas_call x1, Pallas kernels, shards(): pl.pallas_call(functools.partial(kernel, n_dom, n_spec), out_shape=pltpu....  186 us
    pallas_call x1, Pallas kernels, shards(): pl.pallas_call(functools.partial(write_out, n_spec), out_shape=jax.ShapeD...  4.25 us

profile of v8, /device:TPU:15, one launch (start us, length us, event | category | flops | bytes accessed | tf_op | source)
XLA Modules:
  0.0 192.4 jit_solution(16783622345910497508)
XLA Ops:
  0.7 185.6 %shard_map.118.held = f32[32,32768]{1,0:T(8,128)S(1)} custom-call(f32[32,32768]{1,0:T(8,128)} %spectrum.1, f32[256,4096]{1,0:T(8,128)} %cond.1, f32[256,4096]{1,0:T(8,128)} %cap.1, f32[32,128,128]{2,1,0:T(8,128)} %block_cond.1, f32[32,128,128]{2,1,0:T(8,128)} %block_cap.1, s32[1,128]{1,0:T(1,128)} %bound.1, s32[1,3]{1,0:T(1,128)} %sources.1, ...), custom_call_target="tpu_custom_call" | custom-call | flops 6442450944 | bytes 20971520 | tf_op jit(solution)/shard_map/pallas_call | solution.py:336
  186.2 0.0 copy-start
  186.3 1.9 %copy-done = f32[32,32768]{1,0:T(8,128)} copy-done((f32[32,32768]{1,0:T(8,128)}, f32[32,32768]{1,0:T(8,128)S(1)}, u32[]{:S(2)}) %copy-start) | copy-done | bytes 4194328
  188.2 4.3 %shard_map.119 = f32[32,32768]{1,0:T(8,128)} custom-call(f32[32,32768]{1,0:T(8,128)} %copy-done), custom_call_target="tpu_custom_call" | custom-call | tf_op jit(solution)/shard_map/pallas_call | solution.py:390
Async XLA Ops:
  186.2 1.9 %copy-start = (f32[32,32768]{1,0:T(8,128)}, f32[32,32768]{1,0:T(8,128)S(1)}, u32[]{:S(2)}) copy-start(f32[32,32768]{1,0:T(8,128)S(1)} %shard_map.118.held) | copy-start | bytes 12582916
